TPU v7x, 256 devices: a whole 4x4x8 slice. The times are simulated.
256 devices in a mesh: spec: 32 (over x_lo, z, core), bucket: 8 (over y, x_hi).
Axes of the slice: x: 4 (x_hi: 2, x_lo: 2; x = x_hi * 2 + x_lo), y: 4, z: 8, core: 2. Of those that a mesh axis runs over, the one named last changes fastest.
Arguments:
- spectra: bfloat16 [2048, 65536], P('bucket', 'spec'), may hold values from 0 to 20
- theory: bfloat16 [512, 65536], P('bucket', 'spec'), may hold values from 0 to 16
- cand: int32 [2048, 128], P('bucket'), may hold values from 0 to 511
- half: int32 [128], P('spec'), may hold values from 25 to 75
Outputs:
- cand_scores: float32 [2048, 128], P('bucket')
- peptide_score: float32 [512], P(('spec', 'bucket'))
All inputs are finite; a program needn't handle non-finite values.
Results may differ from a plain program's by a relative error of at most 0.0041.
Values may be sent and summed in bfloat16 or wider, within the bound.
No kernel may reach another device: no remote copies, remote signals or barrier semaphores. Data moves between devices by JAX's collectives and lax.ppermute only.
A program may use at most 64 MiB of HBM per device.

v0:
```python
import jax
import jax.numpy as jnp
from jax import lax
from jax.sharding import PartitionSpec as P

HALF = 75
REGION = 512


def extended_2(block, sides, width):
    for axis, dim in sides:
        count = lax.axis_size(axis)
        forward = [(i, i + 1) for i in range(count - 1)]
        backward = [(target, source) for source, target in forward]
        low = lax.ppermute(
            lax.slice_in_dim(block, block.shape[dim] - width, None, axis=dim), axis, forward
        )
        high = lax.ppermute(lax.slice_in_dim(block, 0, width, axis=dim), axis, backward)
        block = jnp.concatenate([low, block, high], axis=dim)
    return block


def broadcast(value, axis, source):
    kept = jnp.where(lax.axis_index(axis) == source, value, 0).astype(value.dtype)
    return lax.psum(kept, axis)


def make_band(widths):
    block_iota = lax.broadcasted_iota(jnp.int32, (3, 128, 128), 0)
    input_iota = lax.broadcasted_iota(jnp.int32, (3, 128, 128), 1)
    output_iota = lax.broadcasted_iota(jnp.int32, (3, 128, 128), 2)
    offset = 128 * (block_iota - 1) + input_iota - output_iota
    return jnp.abs(offset)[None] <= widths[:, None, None, None]


def zscores(score_tile, cand_ids):
    average = jnp.mean(score_tile, axis=1, keepdims=True)
    spread = jnp.mean(jnp.square(score_tile - average), axis=1, keepdims=True)
    picked = jnp.take_along_axis(score_tile, cand_ids, axis=1)
    return (picked - average) * lax.rsqrt(spread + 1e-06)


def against(processed, received):
    return lax.dot_general(
        processed, received, (((1,), (1,)), ((), ())), preferred_element_type=jnp.float32
    )


def on_device(spectra, theory, cand, half):
    row_count, bin_count = spectra.shape
    spec_count = lax.axis_size("spec")
    bucket_count = lax.axis_size("bucket")
    per_bucket = theory.shape[0]
    peptides_all = per_bucket * bucket_count
    position = lax.axis_index("spec")
    extended = extended_2(spectra, (("spec", 1),), HALF)
    bin_widths = jnp.repeat(half, REGION)
    tile_count = bin_count // 128
    padded = jnp.pad(extended, ((0, 0), (128 - HALF, 128 - HALF)))
    tile_view = padded.reshape(row_count, tile_count + 2, 128)
    band_weights = make_band(jnp.repeat(half, REGION // 128)).astype(jnp.bfloat16)
    window_sums = jnp.zeros((row_count, tile_count, 128), jnp.float32)
    for k in range(3):
        window_sums = window_sums + jnp.einsum(
            "rtc,tcd->rtd",
            tile_view[:, k : k + tile_count],
            band_weights[:, k],
            preferred_element_type=jnp.float32,
        )
    window_sums = window_sums.reshape(row_count, bin_count)
    divisor = (2 * bin_widths + 1).astype(jnp.float32)
    processed = (spectra.astype(jnp.float32) - window_sums / divisor).astype(jnp.bfloat16)
    zero_tile = jnp.zeros((row_count, peptides_all), jnp.float32)

    def rooted_step(step_index, running):
        received = broadcast(theory, "bucket", step_index)
        return lax.dynamic_update_slice(
            running, against(processed, received), (jnp.int32(0), step_index * per_bucket)
        )

    score_tile = lax.fori_loop(0, bucket_count, rooted_step, zero_tile)
    summed = lax.psum(score_tile, "spec")
    cand_scores = zscores(summed, cand)
    col_share = cand.shape[1] // spec_count
    local_ids = lax.dynamic_slice_in_dim(cand, position * col_share, col_share, 1)
    local_scores = lax.dynamic_slice_in_dim(cand_scores, position * col_share, col_share, 1)
    partial_value = jax.ops.segment_sum(
        jax.nn.softplus(local_scores).reshape(-1), local_ids.reshape(-1), num_segments=peptides_all
    )
    mean_load = cand.shape[1] * row_count / per_bucket
    peptide_score = (
        lax.psum_scatter(partial_value, ("spec", "bucket"), scatter_dimension=0, tiled=True)
        / mean_load
    )
    return (cand_scores, peptide_score)


def solution(mesh):
    return jax.shard_map(
        on_device,
        mesh=mesh,
        in_specs=(P("bucket", "spec"), P("bucket", "spec"), P("bucket", None), P("spec")),
        out_specs=(P("bucket", None), P(("spec", "bucket"))),
        check_vma=False,
    )
```

profile of v0, /device:TPU:1, one launch (start us, length us, event | category | flops | bytes accessed | tf_op | source)
XLA Modules:
  0.0 1349.8 jit_solution(1085945206522732928)
XLA Ops:
  8.0 1.5 copy.14
  9.6 4.9 collective-permute-start
  14.5 1.9 collective-permute-start.1
  16.4 0.1 subtract_abs_fusion
  16.6 0.1 broadcast_in_dim.32
  16.6 0.1 le.27
  16.7 0.1 broadcast_bitcast_fusion
  16.8 0.5 broadcast_compare_fusion
  17.3 0.1 constant_dynamic-slice_fusion
  17.4 0.1 reshape.69
  17.6 2.2 collective-permute-done.1
  19.8 1.4 concatenate.3
  21.3 0.3 pad.4
  21.6 0.4 fusion.2
  22.0 0.4 fusion.4
  22.4 1.8 add_add_fusion
  24.3 1.9 copy.20
  26.2 1.6 subtract_convert_fusion
  27.9 737.3 %while.15 = (s32[]{:T(128)}, f32[256,512]{0,1:T(8,128)S(1)}, bf16[64,2048]{1,0:T(8,128)(2,1)S(1)}, bf16[256,2048]{1,0:T(8,128)(2,1)S(1)}, s32[]{:T(128)}, /*index=5*/s32[]{:T(128)}, s32[]{:T(128)}, s32[]{:T(128)}, u32[]{:T(128)}) while((s32[]{:T(128)}, f32[256,512]{0,1:T(8,128)S(1)}, bf16[64,2048]{1,0:T(8,128)(2,1)S(1)}, ...), condition=%wide.region_2.3_spmd, body=%wide.region_0.2_spmd.sunk | while | flops 67371016 | bytes 3473621 | solution.py:81
  27.9 0.0 all-reduce.7.cloned.1.call-start
  28.0 0.7 broadcast_select_fusion.2
  28.7 89.5 %all-reduce.7.cloned.1.call-done = bf16[64,2048]{1,0:T(8,128)(2,1)} async-done(((bf16[64,2048]{1,0:T(8,128)(2,1)}), bf16[64,2048]{1,0:T(8,128)(2,1)}) %all-reduce.7.cloned.1.call-update) | async-done | bytes 262160 | tf_op jit(solution)/shard_map/while/body/eval_jaxpr/psum | solution.py:25
  118.2 1.4 fusion.19
  119.6 0.0 all-reduce.7.cloned.1.call-start
  119.6 0.7 broadcast_select_fusion.2
  120.4 90.1 %all-reduce.7.cloned.1.call-done = bf16[64,2048]{1,0:T(8,128)(2,1)} async-done(((bf16[64,2048]{1,0:T(8,128)(2,1)}), bf16[64,2048]{1,0:T(8,128)(2,1)}) %all-reduce.7.cloned.1.call-update) | async-done | bytes 262160 | tf_op jit(solution)/shard_map/while/body/eval_jaxpr/psum | solution.py:25
  210.5 1.4 fusion.19
  211.9 0.0 all-reduce.7.cloned.1.call-start
  212.0 0.7 broadcast_select_fusion.2
  212.8 90.1 %all-reduce.7.cloned.1.call-done = bf16[64,2048]{1,0:T(8,128)(2,1)} async-done(((bf16[64,2048]{1,0:T(8,128)(2,1)}), bf16[64,2048]{1,0:T(8,128)(2,1)}) %all-reduce.7.cloned.1.call-update) | async-done | bytes 262160 | tf_op jit(solution)/shard_map/while/body/eval_jaxpr/psum | solution.py:25
  302.9 1.4 fusion.19
  304.3 0.0 all-reduce.7.cloned.1.call-start
  304.4 0.7 broadcast_select_fusion.2
  305.1 89.8 %all-reduce.7.cloned.1.call-done = bf16[64,2048]{1,0:T(8,128)(2,1)} async-done(((bf16[64,2048]{1,0:T(8,128)(2,1)}), bf16[64,2048]{1,0:T(8,128)(2,1)}) %all-reduce.7.cloned.1.call-update) | async-done | bytes 262160 | tf_op jit(solution)/shard_map/while/body/eval_jaxpr/psum | solution.py:25
  394.9 1.4 fusion.19
  396.3 0.0 all-reduce.7.cloned.1.call-start
  396.4 0.7 broadcast_select_fusion.2
  397.2 89.8 %all-reduce.7.cloned.1.call-done = bf16[64,2048]{1,0:T(8,128)(2,1)} async-done(((bf16[64,2048]{1,0:T(8,128)(2,1)}), bf16[64,2048]{1,0:T(8,128)(2,1)}) %all-reduce.7.cloned.1.call-update) | async-done | bytes 262160 | tf_op jit(solution)/shard_map/while/body/eval_jaxpr/psum | solution.py:25
  487.0 1.4 fusion.19
  488.4 0.0 all-reduce.7.cloned.1.call-start
  488.5 0.7 broadcast_select_fusion.2
  489.2 89.8 %all-reduce.7.cloned.1.call-done = bf16[64,2048]{1,0:T(8,128)(2,1)} async-done(((bf16[64,2048]{1,0:T(8,128)(2,1)}), bf16[64,2048]{1,0:T(8,128)(2,1)}) %all-reduce.7.cloned.1.call-update) | async-done | bytes 262160 | tf_op jit(solution)/shard_map/while/body/eval_jaxpr/psum | solution.py:25
  579.0 1.4 fusion.19
  580.4 0.0 all-reduce.7.cloned.1.call-start
  580.5 0.7 broadcast_select_fusion.2
  581.3 90.1 %all-reduce.7.cloned.1.call-done = bf16[64,2048]{1,0:T(8,128)(2,1)} async-done(((bf16[64,2048]{1,0:T(8,128)(2,1)}), bf16[64,2048]{1,0:T(8,128)(2,1)}) %all-reduce.7.cloned.1.call-update) | async-done | bytes 262160 | tf_op jit(solution)/shard_map/while/body/eval_jaxpr/psum | solution.py:25
  671.4 1.4 fusion.19
  672.8 0.0 all-reduce.7.cloned.1.call-start
  672.9 0.7 broadcast_select_fusion.2
  673.6 90.1 %all-reduce.7.cloned.1.call-done = bf16[64,2048]{1,0:T(8,128)(2,1)} async-done(((bf16[64,2048]{1,0:T(8,128)(2,1)}), bf16[64,2048]{1,0:T(8,128)(2,1)}) %all-reduce.7.cloned.1.call-update) | async-done | bytes 262160 | tf_op jit(solution)/shard_map/while/body/eval_jaxpr/psum | solution.py:25
  763.8 1.4 fusion.19
  765.2 0.0 all-reduce.5.cloned.1.call-start
  765.2 0.7 copy-done.2
  766.0 0.0 all-reduce.5.cloned.1.call-update
  766.1 227.0 %all-reduce.5.cloned.1.call-done = f32[256,512]{0,1:T(8,128)} async-done(((f32[256,512]{0,1:T(8,128)}), f32[256,512]{0,1:T(8,128)}) %all-reduce.5.cloned.1.call-update) | async-done | bytes 524304 | tf_op jit(solution)/shard_map/psum | solution.py:82
  993.0 1.2 reduce_sum.18
  994.2 1.1 multiply_reduce_fusion
  995.4 260.6 %gather_fusion = f32[32768]{0:T(1024)S(1)} fusion(f32[256,512]{0,1:T(8,128)S(1)} %copy-done, s32[32768]{0:T(1024)S(1)} %fusion.8), kind=kCustom, calls=%fused_computation | custom fusion | bytes 524288 | tf_op jit(solution)/shard_map/jit(take_along_axis)/gather | solution.py:39
  1256.0 0.1 fusion.7
  1256.1 0.2 compare_select_fusion
  1256.3 0.1 reshape.71
  1256.4 7.6 scatter_custom_fusion
  1264.0 77.8 %all-reduce.1 = f32[512]{0:T(512)S(1)} all-reduce(f32[512]{0:T(512)S(1)} %scatter_custom_fusion), channel_id=2, replica_groups=mesh['spec'=32,'bucket'=8] {'spec','bucket'}, use_global_device_ids=true, to_apply=%region_7.8.clone | all-reduce | flops 512 | bytes 4096
  1341.8 0.6 dynamic-slice_multiply_fusion
  (28 shorter events, 0.3 us)
Async XLA Ops:
  8.0 8.6 copy-start.5
  8.0 9.3 copy-start.3
  9.6 8.0 collective-permute-start
  14.5 5.3 collective-permute-start.1
  26.2 1.7 copy-start.1
  27.9 90.3 %all-reduce.7.cloned.1.call-start = ((), (), s32[]{:S(2)}) async-start(), calls=%async_computation.1 | async-start | bytes 524288 | tf_op jit(solution)/shard_map/while/body/eval_jaxpr/psum | solution.py:25
  119.6 91.0 %all-reduce.7.cloned.1.call-start = ((), (), s32[]{:S(2)}) async-start(), calls=%async_computation.1 | async-start | bytes 524288 | tf_op jit(solution)/shard_map/while/body/eval_jaxpr/psum | solution.py:25
  211.9 91.0 %all-reduce.7.cloned.1.call-start = ((), (), s32[]{:S(2)}) async-start(), calls=%async_computation.1 | async-start | bytes 524288 | tf_op jit(solution)/shard_map/while/body/eval_jaxpr/psum | solution.py:25
  304.3 90.6 %all-reduce.7.cloned.1.call-start = ((), (), s32[]{:S(2)}) async-start(), calls=%async_computation.1 | async-start | bytes 524288 | tf_op jit(solution)/shard_map/while/body/eval_jaxpr/psum | solution.py:25
  396.3 90.6 %all-reduce.7.cloned.1.call-start = ((), (), s32[]{:S(2)}) async-start(), calls=%async_computation.1 | async-start | bytes 524288 | tf_op jit(solution)/shard_map/while/body/eval_jaxpr/psum | solution.py:25
  488.4 90.6 %all-reduce.7.cloned.1.call-start = ((), (), s32[]{:S(2)}) async-start(), calls=%async_computation.1 | async-start | bytes 524288 | tf_op jit(solution)/shard_map/while/body/eval_jaxpr/psum | solution.py:25
  580.4 91.0 %all-reduce.7.cloned.1.call-start = ((), (), s32[]{:S(2)}) async-start(), calls=%async_computation.1 | async-start | bytes 524288 | tf_op jit(solution)/shard_map/while/body/eval_jaxpr/psum | solution.py:25
  672.8 91.0 %all-reduce.7.cloned.1.call-start = ((), (), s32[]{:S(2)}) async-start(), calls=%async_computation.1 | async-start | bytes 524288 | tf_op jit(solution)/shard_map/while/body/eval_jaxpr/psum | solution.py:25
  765.2 0.8 copy-start.2
  765.2 227.9 %all-reduce.5.cloned.1.call-start = ((), (), s32[]{:S(2)}) async-start(), calls=%async_computation | async-start | bytes 1048576 | tf_op jit(solution)/shard_map/psum | solution.py:82
  993.0 2.4 copy-start
  1256.1 86.3 %copy-start.4 = (f32[256,128]{1,0:T(8,128)}, f32[256,128]{1,0:T(8,128)S(1)}, u32[]{:S(2)}) copy-start(f32[256,128]{1,0:T(8,128)S(1)} %fusion.7) | copy-start | bytes 393220
Sparse Core Ops, SparseCore 0:
  31.5 86.5 all-reduce.6
  123.2 87.2 all-reduce.6
  215.6 87.2 all-reduce.6
  307.6 87.2 all-reduce.6
  399.7 87.2 all-reduce.6
  491.7 87.2 all-reduce.6
  584.1 87.2 all-reduce.6
  676.4 87.2 all-reduce.6
Sparse Core Ops, SparseCore 1:
  768.3 224.7 all-reduce.4
where the time goes:
time: 1350 us
  waiting for transfers between devices  949 us (70%)
  local copies, waits for them, and re-layouts  267 us (20%)
  blocking collectives  77.8 us (6%)
  other arithmetic  18.9 us (1%)
  between operations  15.7 us (1%)
  matrix products  13.8 us (1%)
    psum x8, waiting for transfers between devices, broadcast(): return lax.psum(kept, axis)  720 us
    gather x1, local copies, waits for them, and re-layouts, zscores(): picked = jnp.take_along_axis(score_tile, cand_ids, axis=1)  261 us
    psum x1, waiting for transfers between devices, on_device(): summed = lax.psum(score_tile, 'spec')  227 us
    unnamed x1, blocking collectives  77.8 us
  transfers between devices with their start and end apart: 11, of which 10 were waited for; matrix products, arithmetic and copies ran while one was open for 0% of the time, Pallas kernels for 0%

commit v1 on v0

--- a/solution.py
+++ b/solution.py
@@ -5,6 +5,12 @@
 
 HALF = 75
 REGION = 512
+
+
+def gather_and_add(shard, axis):
+    shards = lax.all_gather(shard, axis, axis=0, tiled=False)
+    result = shards.sum(axis=0)
+    return result
 
 
 def extended_2(block, sides, width):
@@ -79,7 +85,7 @@
         )
 
     score_tile = lax.fori_loop(0, bucket_count, rooted_step, zero_tile)
-    summed = lax.psum(score_tile, "spec")
+    summed = gather_and_add(score_tile, "spec")
     cand_scores = zscores(summed, cand)
     col_share = cand.shape[1] // spec_count
     local_ids = lax.dynamic_slice_in_dim(cand, position * col_share, col_share, 1)

time: 1350 us -> 1260 us (0.933)
  waiting for transfers between devices: 949 us -> 824 us
  local copies, waits for them, and re-layouts: 267 us -> 283 us
    psum x1 -> x0, waiting for transfers between devices: 227 us -> none  [on_device(): summed = lax.psum(score_tile, 'spec')]
    all_gather x0 -> x1, waiting for transfers between devices: none -> 104 us  [gather_and_add(): shards = lax.all_gather(shard, axis, axis=0, tiled=False)]
    unnamed x15 -> x14, local copies, waits for them, and re-layouts: 2.36 us -> 18 us
where the time goes in v1:
time: 1260 us; the launch traced here: 1250 us
  waiting for transfers between devices  824 us (65%)
  local copies, waits for them, and re-layouts  283 us (22%)
  blocking collectives  78.1 us (6%)
  other arithmetic  31.9 us (3%)
  between operations  15.7 us (1%)
  matrix products  13.8 us (1%)
    psum x8, waiting for transfers between devices, broadcast(): return lax.psum(kept, axis)  720 us
    gather x1, local copies, waits for them, and re-layouts, zscores(): picked = jnp.take_along_axis(score_tile, cand_ids, axis=1)  261 us
    all_gather x1, waiting for transfers between devices, gather_and_add(): shards = lax.all_gather(shard, axis, axis=0, tiled=False)  104 us
    unnamed x1, blocking collectives  78.1 us
  transfers between devices with their start and end apart: 11, of which 10 were waited for; matrix products, arithmetic and copies ran while one was open for 0% of the time, Pallas kernels for 0%

profile of v1, /device:TPU:1, one launch (start us, length us, event | category | flops | bytes accessed | tf_op | source)
XLA Modules:
  0.0 1254.8 jit_solution(283753409662075569)
XLA Ops:
  8.0 1.5 copy.29
  9.5 5.1 collective-permute-start.1
  14.7 1.9 collective-permute-start
  16.6 0.1 broadcast_in_dim.32
  16.7 0.1 le.27
  16.8 0.1 subtract_abs_fusion
  16.9 0.5 broadcast_compare_fusion
  17.4 0.1 broadcast_bitcast_fusion
  17.5 0.3 collective-permute-done
  17.8 1.4 concatenate.3
  19.2 0.3 pad.4
  19.5 0.4 fusion.2
  20.0 0.4 fusion.4
  20.4 1.8 add_add_fusion
  22.2 1.9 copy.35
  24.2 1.6 subtract_convert_fusion
  25.9 737.4 %while.15 = (s32[]{:T(128)}, f32[256,512]{0,1:T(8,128)S(1)}, bf16[64,2048]{1,0:T(8,128)(2,1)S(1)}, bf16[256,2048]{1,0:T(8,128)(2,1)S(1)}, s32[]{:T(128)}, /*index=5*/s32[]{:T(128)}, s32[]{:T(128)}, s32[]{:T(128)}, u32[]{:T(128)}) while((s32[]{:T(128)}, f32[256,512]{0,1:T(8,128)S(1)}, bf16[64,2048]{1,0:T(8,128)(2,1)S(1)}, ...), condition=%wide.region_2.3_spmd, body=%wide.region_0.2_spmd.sunk | while | flops 67371016 | bytes 3473629 | solution.py:87
  25.9 0.0 all-reduce.4.cloned.1.call-start
  25.9 0.7 broadcast_select_fusion.2
  26.7 90.9 %all-reduce.4.cloned.1.call-done = bf16[64,2048]{1,0:T(8,128)(2,1)} async-done(((bf16[64,2048]{1,0:T(8,128)(2,1)}), bf16[64,2048]{1,0:T(8,128)(2,1)}) %all-reduce.4.cloned.1.call-update) | async-done | bytes 262160 | tf_op jit(solution)/shard_map/while/body/eval_jaxpr/psum | solution.py:31
  117.6 1.4 fusion.19
  119.0 0.0 all-reduce.4.cloned.1.call-start
  119.1 0.7 broadcast_select_fusion.2
  119.8 90.0 %all-reduce.4.cloned.1.call-done = bf16[64,2048]{1,0:T(8,128)(2,1)} async-done(((bf16[64,2048]{1,0:T(8,128)(2,1)}), bf16[64,2048]{1,0:T(8,128)(2,1)}) %all-reduce.4.cloned.1.call-update) | async-done | bytes 262160 | tf_op jit(solution)/shard_map/while/body/eval_jaxpr/psum | solution.py:31
  209.8 1.4 fusion.19
  211.2 0.0 all-reduce.4.cloned.1.call-start
  211.3 0.7 broadcast_select_fusion.2
  212.0 89.9 %all-reduce.4.cloned.1.call-done = bf16[64,2048]{1,0:T(8,128)(2,1)} async-done(((bf16[64,2048]{1,0:T(8,128)(2,1)}), bf16[64,2048]{1,0:T(8,128)(2,1)}) %all-reduce.4.cloned.1.call-update) | async-done | bytes 262160 | tf_op jit(solution)/shard_map/while/body/eval_jaxpr/psum | solution.py:31
  302.0 1.4 fusion.19
  303.4 0.0 all-reduce.4.cloned.1.call-start
  303.4 0.7 broadcast_select_fusion.2
  304.2 89.6 %all-reduce.4.cloned.1.call-done = bf16[64,2048]{1,0:T(8,128)(2,1)} async-done(((bf16[64,2048]{1,0:T(8,128)(2,1)}), bf16[64,2048]{1,0:T(8,128)(2,1)}) %all-reduce.4.cloned.1.call-update) | async-done | bytes 262160 | tf_op jit(solution)/shard_map/while/body/eval_jaxpr/psum | solution.py:31
  393.8 1.4 fusion.19
  395.2 0.0 all-reduce.4.cloned.1.call-start
  395.3 0.7 broadcast_select_fusion.2
  396.0 89.6 %all-reduce.4.cloned.1.call-done = bf16[64,2048]{1,0:T(8,128)(2,1)} async-done(((bf16[64,2048]{1,0:T(8,128)(2,1)}), bf16[64,2048]{1,0:T(8,128)(2,1)}) %all-reduce.4.cloned.1.call-update) | async-done | bytes 262160 | tf_op jit(solution)/shard_map/while/body/eval_jaxpr/psum | solution.py:31
  485.7 1.4 fusion.19
  487.1 0.0 all-reduce.4.cloned.1.call-start
  487.1 0.7 broadcast_select_fusion.2
  487.9 89.6 %all-reduce.4.cloned.1.call-done = bf16[64,2048]{1,0:T(8,128)(2,1)} async-done(((bf16[64,2048]{1,0:T(8,128)(2,1)}), bf16[64,2048]{1,0:T(8,128)(2,1)}) %all-reduce.4.cloned.1.call-update) | async-done | bytes 262160 | tf_op jit(solution)/shard_map/while/body/eval_jaxpr/psum | solution.py:31
  577.5 1.4 fusion.19
  578.9 0.0 all-reduce.4.cloned.1.call-start
  579.0 0.7 broadcast_select_fusion.2
  579.7 90.0 %all-reduce.4.cloned.1.call-done = bf16[64,2048]{1,0:T(8,128)(2,1)} async-done(((bf16[64,2048]{1,0:T(8,128)(2,1)}), bf16[64,2048]{1,0:T(8,128)(2,1)}) %all-reduce.4.cloned.1.call-update) | async-done | bytes 262160 | tf_op jit(solution)/shard_map/while/body/eval_jaxpr/psum | solution.py:31
  669.7 1.4 fusion.19
  671.2 0.7 broadcast_select_fusion.2
  671.9 90.0 %all-reduce.4.cloned.1.call-done = bf16[64,2048]{1,0:T(8,128)(2,1)} async-done(((bf16[64,2048]{1,0:T(8,128)(2,1)}), bf16[64,2048]{1,0:T(8,128)(2,1)}) %all-reduce.4.cloned.1.call-update) | async-done | bytes 262160 | tf_op jit(solution)/shard_map/while/body/eval_jaxpr/psum | solution.py:31
  761.9 1.4 fusion.19
  763.3 0.2 all-gather.3.cloned.1.call-start
  763.5 0.5 copy-done.1
  764.1 0.1 constant_dynamic-slice_fusion
  764.2 0.1 reshape.69
  764.4 104.4 %all-gather.3.cloned.1.call-done = f32[8192,512]{0,1:T(8,128)} async-done(((f32[256,512]{0,1:T(8,128)}), f32[8192,512]{0,1:T(8,128)}) %all-gather.3.cloned.1.call-update) | async-done | bytes 16777232 | tf_op jit(solution)/shard_map/all_gather | solution.py:11
  868.8 6.5 reduce.1
  875.4 15.8 %copy.40 = f32[64,8,32,256]{3,2,1,0:T(8,128)} copy(f32[64,8,32,256]{3,1,2,0:T(8,128)} %bitcast.45) | data formatting | bytes 33554432
  891.2 8.7 bitcast_reduce_fusion
  899.9 260.6 %gather_fusion = f32[32768]{0:T(1024)S(1)} fusion(f32[256,512]{0,1:T(8,128)S(1)} %bitcast_reduce_fusion, s32[32768]{0:T(1024)S(1)} %fusion.8), kind=kCustom, calls=%fused_computation | custom fusion | bytes 524288 | tf_op jit(solution)/shard_map/jit(take_along_axis)/gather | solution.py:45
  1160.5 0.1 multiply_reduce_fusion
  1160.6 0.1 fusion.7
  1160.7 0.1 compare_select_fusion
  1160.9 0.1 reshape.71
  1161.0 7.6 scatter_custom_fusion
  1168.6 78.1 %all-reduce.1 = f32[512]{0:T(512)S(1)} all-reduce(f32[512]{0:T(512)S(1)} %scatter_custom_fusion), channel_id=3, replica_groups=mesh['spec'=32,'bucket'=8] {'spec','bucket'}, use_global_device_ids=true, to_apply=%region_7.8.clone | all-reduce | flops 512 | bytes 4096
  1246.8 0.6 dynamic-slice_multiply_fusion
  (30 shorter events, 0.4 us)
Async XLA Ops:
  8.0 8.6 copy-start.4
  9.5 8.0 collective-permute-start.1
  14.7 3.1 collective-permute-start
  24.2 1.7 copy-start
  25.8 738.3 %copy-start.2 = (s32[256,128]{1,0:T(8,128)S(1)}, s32[256,128]{1,0:T(8,128)}, u32[]{:S(2)}) copy-start(s32[256,128]{1,0:T(8,128)} %param.8) | copy-start | bytes 393220
  25.9 91.8 %all-reduce.4.cloned.1.call-start = ((), (), s32[]{:S(2)}) async-start(), calls=%async_computation.1 | async-start | bytes 524288 | tf_op jit(solution)/shard_map/while/body/eval_jaxpr/psum | solution.py:31
  119.0 90.8 %all-reduce.4.cloned.1.call-start = ((), (), s32[]{:S(2)}) async-start(), calls=%async_computation.1 | async-start | bytes 524288 | tf_op jit(solution)/shard_map/while/body/eval_jaxpr/psum | solution.py:31
  211.2 90.8 %all-reduce.4.cloned.1.call-start = ((), (), s32[]{:S(2)}) async-start(), calls=%async_computation.1 | async-start | bytes 524288 | tf_op jit(solution)/shard_map/while/body/eval_jaxpr/psum | solution.py:31
  303.4 90.5 %all-reduce.4.cloned.1.call-start = ((), (), s32[]{:S(2)}) async-start(), calls=%async_computation.1 | async-start | bytes 524288 | tf_op jit(solution)/shard_map/while/body/eval_jaxpr/psum | solution.py:31
  395.2 90.5 %all-reduce.4.cloned.1.call-start = ((), (), s32[]{:S(2)}) async-start(), calls=%async_computation.1 | async-start | bytes 524288 | tf_op jit(solution)/shard_map/while/body/eval_jaxpr/psum | solution.py:31
  487.1 90.5 %all-reduce.4.cloned.1.call-start = ((), (), s32[]{:S(2)}) async-start(), calls=%async_computation.1 | async-start | bytes 524288 | tf_op jit(solution)/shard_map/while/body/eval_jaxpr/psum | solution.py:31
  578.9 90.8 %all-reduce.4.cloned.1.call-start = ((), (), s32[]{:S(2)}) async-start(), calls=%async_computation.1 | async-start | bytes 524288 | tf_op jit(solution)/shard_map/while/body/eval_jaxpr/psum | solution.py:31
  671.1 90.8 %all-reduce.4.cloned.1.call-start = ((), (), s32[]{:S(2)}) async-start(), calls=%async_computation.1 | async-start | bytes 524288 | tf_op jit(solution)/shard_map/while/body/eval_jaxpr/psum | solution.py:31
  763.3 0.8 copy-start.1
  763.3 105.5 %all-gather.3.cloned.1.call-start = ((), (), s32[]{:S(2)}) async-start(), calls=%async_computation | async-start | bytes 17301504 | tf_op jit(solution)/shard_map/all_gather | solution.py:11
  1160.7 86.6 %copy-start.3 = (f32[256,128]{1,0:T(8,128)}, f32[256,128]{1,0:T(8,128)S(1)}, u32[]{:S(2)}) copy-start(f32[256,128]{1,0:T(8,128)S(1)} %fusion.7) | copy-start | bytes 393220
Sparse Core Ops, SparseCore 0:
  29.3 88.2 all-reduce.3
  122.5 87.2 all-reduce.3
  214.6 87.2 all-reduce.3
  306.5 87.2 all-reduce.3
  398.4 87.2 all-reduce.3
  490.2 87.2 all-reduce.3
  582.4 87.2 all-reduce.3
  674.6 87.2 all-reduce.3
Sparse Core Ops, SparseCore 1:
  765.6 103.1 all-gather.2
